TPU v7x, 32 devices: a whole 2x2x4 slice. The times are simulated.
32 devices in a mesh: clip: 32 (over z, y, x, core).
Axes of the slice: x: 2, y: 2, z: 4, core: 2. Of those that a mesh axis runs over, the one named last changes fastest.
Arguments:
- frames: bfloat16 [128, 14, 14, 1024], P('clip'), may hold values from -6 to 6
- w_reduce: bfloat16 [1024, 256], replicated, may hold values from -0.1875 to 0.1875
- w_spatial: bfloat16 [3, 3, 256, 256], replicated, may hold values from -0.125 to 0.125
- w_expand: bfloat16 [256, 1024], replicated, may hold values from -0.375 to 0.375
- gain_a: float32 [256], replicated, may hold values from 0.5 to 1.5
- bias_a: float32 [256], replicated, may hold values from -3 to 3
- gain_b: float32 [256], replicated, may hold values from 0.5 to 1.5
- bias_b: float32 [256], replicated, may hold values from -3 to 3
- gain_c: float32 [1024], replicated, may hold values from 0.5 to 1.5
- bias_c: float32 [1024], replicated, may hold values from -3 to 3
- clip_ids: int32 [128], P('clip'), may hold values from 0 to 31, as said below
- segment_ids: int32 [128], P('clip'), may hold values from 0 to 2
- slot_valid: int32 [128], P('clip'), may hold values from 0 to 1, as said below
- segment_weight: float32 [3], replicated, may hold values from 0.5 to 2
- loss_weight: float32 [1024], replicated, may hold values from -3600 to 3600
Outputs:
- grad_frames: bfloat16 [128, 14, 14, 1024], P('clip')
- grad_reduce: float32 [1024, 256], replicated
- grad_spatial: float32 [3, 3, 256, 256], replicated
- grad_expand: float32 [256, 1024], replicated
- grad_gain_a: float32 [256], replicated
- grad_bias_a: float32 [256], replicated
- grad_gain_b: float32 [256], replicated
- grad_bias_b: float32 [256], replicated
- grad_gain_c: float32 [1024], replicated
- grad_bias_c: float32 [1024], replicated
Inputs may be any that keep to these rules, and one draw needn't show every extreme that they name: `clip_ids`: every clip has exactly 3 slots, one of each segment index, on the devices d, d + 1 and d + D/2 (mod D, where D is the number of devices along `clip` in the mesh's order) for some d; which segment sits on which of those devices varies by draw. Each device holds exactly 3 such slots and its other slots are padding. `slot_valid`: segment 0 of every clip is valid; padding slots are not.
All inputs are finite; a program needn't handle non-finite values.
Results may differ from a plain program's by a relative error of at most 0.007.
Values sent between devices are 32-bit elements; how exact they have to be, the bound alone decides.
A program may use at most 128 MiB of HBM per device.

v0:
```python
import functools
from types import SimpleNamespace

import jax
import jax.numpy as jnp
from jax import lax
from jax.experimental import pallas as pl
from jax.experimental.pallas import tpu as pltpu
from jax.sharding import PartitionSpec as P

MESH = pl.DeviceIdType.MESH
EPS = 1e-05
F32 = jnp.float32
BF16 = jnp.bfloat16
SIDE = 16
ROWS = SIDE * SIDE
NN = (((1,), (0,)), ((), ()))
NT = (((1,), (1,)), ((), ()))

ORDER = (
    (),
    (),
    (),
    (),
    (),
    (),
    (0, 1,),
    (2, 0,),
    (1,),
    (2, 0, 1, 3,),
    (2, 4,),
    (),
    (),
    (0,),
    (1, 3, 5, 2, 4,),
    (6, 3, 8,),
    (1, 0, 5, 7, 4, 8, 1, 3, 6, 7, 8, 2, 0,),
    (4, 7, 3,),
    (6, 2, 8, 1, 5, 0, 4, 7, 3, 6, 8, 5, 7, 1, 6, 4,),
    (5, 6, 0, 3,),
    (7,),
    (8, 2, 4, 5, 7, 8, 6, 3, 5,),
    (7, 8, 6, 5, 4, 2,),
)


def dot(a, b, dims=NN):
    return lax.dot_general(a, b, dims, preferred_element_type=F32)


def wait_bytes(ref, sem):
    pltpu.make_async_copy(ref, ref, sem).wait()


def by_rows(ref, value):
    for k in range(ref.shape[0] // 256):
        ref[k * 256 : (k + 1) * 256, :] = value(slice(k * 256, (k + 1) * 256))


def moved_rows(here, at):
    return slice(here.start + at, here.stop + at)


def block(k, y):
    return pl.multiple_of(k * ROWS + y * SIDE, SIDE)


def to_dense(ref, at, value, first):
    for q in range(value.shape[1] // 128):
        ref[at, pl.ds(first + q, 1), :] = value[:, q * 128 : (q + 1) * 128]


def row_form(ref, row, source, first, count, lane=0):
    for q in range(count):
        ref[row : row + 1, (lane + q) * 128 : (lane + q + 1) * 128] = source[first + q : first + q + 1, :]


def three(ref, at, left, middle, right):
    here, wide = pl.ds(at + SIDE, SIDE), middle.shape[1]
    ref[here, 0:wide] = left.astype(BF16)
    ref[here, wide : 2 * wide] = middle.astype(BF16)
    ref[here, 2 * wide : 3 * wide] = right.astype(BF16)


def dense_of(ref1, scratch):
    count = ref1.shape[0] // 128
    for q in range(count):
        scratch[q : q + 1, :] = ref1[q * 128 : (q + 1) * 128].reshape(1, 128)
    return scratch[0:count, :]


class Step:
    def __init__(self, cfg, r):
        self.r, self.sizes = r, cfg
        self.n, self.slots, self.height, self.width, self.feat, self.mid = cfg
        self.live = self.slots - 1
        self.rows = self.live * ROWS
        self.area = self.height * self.width
        self.inner = 8
        self.outer = self.n // 8
        self.quad = min(4, self.outer)
        self.far = self.outer // self.quad
        self.loads = {}
        self.mask = lax.broadcasted_iota(jnp.int32, (SIDE, 256), 0) < self.width

    def load(self, **pairs):
        for name, (src, dst) in pairs.items():
            copy = pltpu.make_async_copy(src, dst, self.r.load_sem.at[len(self.loads)])
            copy.start()
            self.loads[name] = copy

    def loaded(self, **names):
        for name in names:
            self.loads[name].wait()

    def fold(self, value):
        return jnp.sum(jnp.where(self.mask, value, 0.0), axis=0, keepdims=True)

    def slot_facts(self):
        r, live = self.r, self.live
        alive, later = 1, []
        for k in range(live):
            alive = alive * r.valid[k]
            later.append(1 - alive)
        self.keep = [(1 - q).astype(F32) for q in later]
        self.moved = [q.astype(F32) for q in later]
        self.later = later
        self.v = [self.kept(r.valid, k) for k in range(live)]
        self.n_own = (self.v[0] + self.v[1] + self.v[2]) * float(self.area)

    def kept(self, values, k):
        return (values[k] + self.later[k] * (values[k + 1] - values[k])).astype(F32)

    def places(self):
        n = self.n
        self.me = me = lax.axis_index("clip")
        self.low, self.high = low, high = me % self.inner, me // self.inner
        self.direct = n <= 32
        self.peers = flips(me, n)
        self.low_peers = flips(me, self.inner)
        self.high_peers = flips(me, self.outer, self.inner)
        self.clip_peers = [(me + o) % n for o in (n // 2 - 1, n // 2 + 1, n // 2, n - 1, 1)]

    def greet(self):
        self.greeted = self.peers if self.direct else self.low_peers + self.high_peers + self.clip_peers
        self.barrier = pltpu.get_barrier_semaphore()
        for device in self.greeted:
            pl.semaphore_signal(self.barrier, inc=1, device_id=(device,), device_id_type=MESH)

    def all_here(self):
        pl.semaphore_wait(self.barrier, len(self.greeted))

    def send(self, src, dst, ssem, rsem, device):
        pltpu.make_async_remote_copy(
            src_ref=src, dst_ref=dst, send_sem=ssem, recv_sem=rsem, device_id=(device,), device_id_type=MESH
        ).start()

    def one_stage(self, at):
        return self.direct and at not in (2, 3, 6)

    def near_at(self, at):
        return self.me if self.one_stage(at) else self.low

    def near_send(self, at):
        buf, mine = self.r.near[at], self.near_at(at)
        for device in self.peers if self.one_stage(at) else self.low_peers:
            self.send(buf.at[mine], buf.at[mine], self.r.near_s.at[at], self.r.near_r.at[at], device)

    def near_wait(self, at, sems):
        buf = self.r.near[at]
        wait_bytes(buf.at[pl.ds(0, buf.shape[0] - 1)], sems.at[at])

    def wide_send(self, at):
        buf = self.r.wide[at]
        for device in self.high_peers:
            self.send(buf.at[self.high], buf.at[self.high], self.r.wide_s.at[at], self.r.wide_r.at[at], device)

    def wide_wait(self, at, sems):
        wait_bytes(self.r.wide[at].at[pl.ds(0, self.outer - 1)], sems.at[at])

    def all_sent(self, *rounds):
        for at in rounds:
            self.near_wait(at, self.r.near_s)
            if not self.one_stage(at):
                self.wide_wait(at, self.r.wide_s)

    def near_count(self, q):
        return self.r.near[0][(self.me - self.low + q) if self.direct else q, 4:5, :]

    def wide_count(self, q):
        return self.r.plane[q, 0:1, :] if self.direct else self.r.wide[0][q, 4:5, :]

    def stats_near(self, at, count):
        if self.one_stage(at):
            return
        self.near_wait(at, self.r.near_r)
        n_all, s_all, _, spread = combine(self.r.near[at], self.near_count, self.inner, count)
        buf = self.r.wide[at]
        buf[self.high, 0:count, :] = s_all
        buf[self.high, count : 2 * count, :] = spread
        if at == 0:
            buf[self.high, 4:5, :] = n_all
        self.wide_send(at)

    def stats_wide(self, at, count, table, first=0):
        r = self.r
        if self.one_stage(at):
            self.near_wait(at, r.near_r)
            counts = r.near[0]
            n_all, _, mean, spread = combine(r.near[at], lambda q: counts[q, 4:5, :], self.n, count)
        else:
            self.wide_wait(at, r.wide_r)
            n_all, _, mean, spread = combine(r.wide[at], self.wide_count, self.outer, count)
        if at == 0 and self.direct:
            counts = r.near[0]
            for q in range(self.outer):
                r.plane[q, 0:1, :] = sum(counts[q * self.inner + m, 4:5, :] for m in range(self.inner))
        inverse = lax.rsqrt(spread / n_all + EPS)
        r.dense[0:count, :] = mean
        row_form(table, 0, r.dense, 0, count, first)
        r.dense[0:count, :] = inverse
        row_form(table, 1, r.dense, 0, count, first)
        return n_all, inverse

    def sums_near(self, at):
        if not self.one_stage(at):
            self.near_wait(at, self.r.near_r)
            self.r.wide[at][self.high] = total(self.r.near[at])
            self.wide_send(at)

    def sums_wide(self, at):
        if self.one_stage(at):
            self.near_wait(at, self.r.near_r)
            return total(self.r.near[at])
        self.wide_wait(at, self.r.wide_r)
        return total(self.r.wide[at])

    def local_stats(self, buf, at, ref, first=0, channels=None):
        channels = channels or ref.shape[1]
        count = channels // 128
        for c in range(channels // 256):
            lanes = slice(first + c * 256, first + (c + 1) * 256)

            def gather(term):
                acc = jnp.zeros((SIDE, 256), F32)
                for k in range(self.live):
                    part = lax.fori_loop(
                        0, self.height, lambda y, a: a + term(ref[pl.ds(block(k, y), SIDE), lanes]),
                        jnp.zeros((SIDE, 256), F32), unroll=self.height,
                    )
                    acc = acc + part * self.v[k]
                return self.fold(acc)

            s_own = gather(lambda x: x)
            mean = s_own / jnp.maximum(self.n_own, 1.0)
            to_dense(buf, at, s_own, 2 * c)
            to_dense(buf, at, gather(lambda x: (x - mean) * (x - mean)), count + 2 * c)

    def norm_silu(self, ref, slope_ref, table, gain, bias, write):
        centre, scale = table[0:1, :], table[1:2, :] * gain[...].reshape(1, self.mid)
        b = bias[...].reshape(1, self.mid)
        for k in range(self.live):
            def step(y, carry):
                at = block(k, y)
                u = (ref[pl.ds(at, SIDE), :] - centre) * scale + b
                s = 0.5 * jnp.tanh(0.5 * u) + 0.5
                h = u * s
                slope_ref[pl.ds(at, SIDE), :] = jnp.where(self.mask, s + (h - h * s), 0.0)
                write(at, jnp.where(self.mask, h, 0.0))
                return carry

            lax.fori_loop(0, self.height, step, 0, unroll=self.height)


def flips(index, count, stride=1):
    steps, at = [], 1
    while at < count:
        steps.append(at * stride * (1 - 2 * ((index // (at * stride)) % 2)))
        at *= 2
    return [sum((d for b, d in enumerate(steps) if o >> b & 1), index) for o in reversed(range(1, count))]


def combine(buf, counts, group, count):
    n_part = [counts(q) for q in range(group)]
    s_part = [buf[q, 0:count, :] for q in range(group)]
    n_all = sum(n_part[1:], n_part[0])
    s_all = sum(s_part[1:], s_part[0])
    mean = s_all / jnp.maximum(n_all, 1.0)
    spread = jnp.zeros((count, 128), F32)
    for q in range(group):
        gap = s_part[q] / jnp.maximum(n_part[q], 1.0) - mean
        spread = spread + (buf[q, count : 2 * count, :] + n_part[q] * gap * gap)
    return n_all, s_all, mean, spread


def total(buf):
    out = buf[0]
    for q in range(1, buf.shape[0]):
        out = out + buf[q]
    return out


def clear(*refs):
    for ref in refs:
        ref[...] = jnp.zeros(ref.shape, ref.dtype)


def prologue(t):
    r, slots, live, width, feat = t.r, t.slots, t.live, t.width, t.feat
    t.places()
    t.greet()
    t.load(
        frames=(r.frames, r.f4.at[pl.ds(0, t.area)]), valid=(r.slot_valid, r.valid), reduce=(r.w_reduce, r.wr)
    )
    r.f4[t.area :] = jnp.zeros((r.f4.shape[0] - t.area, *r.f4.shape[1:]), BF16)
    clear(r.fp)
    t.loaded(valid=0)
    t.slot_facts()
    t.loaded(frames=0)
    t.load(
        clip=(r.clip_ids, r.clip), segment=(r.segment_ids, r.segment),
        share=(r.segment_weight, r.share), spatial=(r.w_spatial, r.ws), expand=(r.w_expand, r.we),
        ga=(r.gain_a, r.ga), ba=(r.bias_a, r.ba), gb=(r.gain_b, r.gb), bb=(r.bias_b, r.bb),
        gc=(r.gain_c, r.gc), bc=(r.bias_c, r.bc), loss=(r.loss_weight, r.loss),
    )
    for i in range(3):
        for j in range(3):
            pltpu.make_async_copy(
                r.w_spatial.at[i, j], r.wc.at[i, :, pl.ds(j * t.mid, t.mid)], r.load_sem.at[15]
            ).start()
    fp, f4 = r.fp, r.f4
    tiles = feat // 128
    group = SIDE // slots
    short = lax.broadcasted_iota(jnp.int32, (SIDE, 128), 0) < width

    def regroup(y, carry):
        for p in range(tiles // group):
            value = f4[pl.ds(y * width, SIDE), p * SIDE : (p + 1) * SIDE, :].astype(F32)
            value = jnp.swapaxes(value, 0, 1)
            for q in range(group):
                for k in range(live):
                    row = value[q * slots + k] * t.keep[k] + value[q * slots + k + 1] * t.moved[k]
                    lanes = slice((p * group + q) * 128, (p * group + q + 1) * 128)
                    fp[pl.ds(block(k, y), SIDE), lanes] = jnp.where(short, row, 0.0).astype(BF16)
        return carry

    lax.fori_loop(0, t.height, regroup, 0)
    t.loaded(reduce=0)
    by_rows(r.pre_a, lambda here: dot(fp[here, :], r.wr[...]))
    t.local_stats(r.near[0], t.near_at(0), r.pre_a)
    r.near[0][t.near_at(0), 4:5, :] = jnp.full((1, 128), t.n_own, F32)


def forward(t):
    r, live, mid, feat, rows, area, height = t.r, t.live, t.mid, t.feat, t.rows, t.area, t.height

    def turn(q):
        lanes = slice(q * feat // 4, (q + 1) * feat // 4)
        r.ft[lanes, :] = r.fp[:, lanes].T

    t.all_here()
    t.near_send(0)
    turn(0)
    t.stats_near(0, mid // 128)
    clear(r.xp, r.hb, r.g3, r.gpc, r.gpa)
    t.loaded(clip=0, segment=0, share=0, ga=0, ba=0, gb=0, bb=0, gc=0, bc=0, loss=0, spatial=0, expand=0)
    key = [t.kept(r.clip, k) for k in range(live)]
    weight = []
    for k in range(live):
        at = t.kept(r.segment, k)
        w0, w1, w2 = (r.share[q] for q in range(3))
        weight.append(
            t.v[k] * (w0 * ((1.0 - at) * (2.0 - at) * 0.5) + w1 * (at * (2.0 - at)) + w2 * (at * (at - 1.0) * 0.5))
        )
    n_all, inv_a = t.stats_wide(0, mid // 128, r.table_a)

    xp, hb = r.xp, r.hb

    def write_a(at, h):
        three(xp, at, pltpu.roll(h, 1, 0), h, pltpu.roll(h, SIDE - 1, 0))

    t.norm_silu(r.pre_a, r.slope_a, r.table_a, r.ga, r.ba, write_a)

    by_rows(
        r.pre_b,
        lambda here: sum(dot(xp[moved_rows(here, i * SIDE), :], r.ws[i].reshape(3 * mid, mid)) for i in range(3)),
    )
    t.local_stats(r.near[1], t.near_at(1), r.pre_b)
    t.near_send(1)
    r.xt[...] = xp[SIDE : SIDE + rows, mid : 2 * mid].T
    t.stats_near(1, mid // 128)
    _, inv_b = t.stats_wide(1, mid // 128, r.table_b)

    def write_b(at, h):
        hb[pl.ds(at, SIDE), :] = h.astype(BF16)

    t.norm_silu(r.pre_b, r.slope_b, r.table_b, r.gb, r.bb, write_b)

    pre_c, slope_c, fp, table_c = r.pre_c, r.slope_c, r.fp, r.table_c
    half = feat // 2
    rounds = (2, 6)
    for h, at in enumerate(rounds):
        lanes = slice(h * half, (h + 1) * half)
        for k in range(live):
            here = slice(k * ROWS, (k + 1) * ROWS)
            pre_c[here, lanes] = dot(hb[here, :], r.we[:, lanes])
        t.local_stats(r.near[at], t.near_at(at), pre_c, h * half, half)
        t.near_send(at)
    r.hbt[...] = hb[...].T
    for at in rounds:
        t.stats_near(at, half // 128)
    turn(1)

    pool, slope_sum, slope_hat = r.pool, r.slope_sum, r.slope_hat
    for c in range(feat // 256):
        if c * 256 % half == 0:
            h = c * 256 // half
            _, inv_half = t.stats_wide(rounds[h], half // 128, table_c, h * half // 128)
            r.inv_c[h * half // 128 : (h + 1) * half // 128, :] = inv_half
        lanes = slice(c * 256, (c + 1) * 256)
        centre, inverse = table_c[0:1, lanes], table_c[1:2, lanes]
        g = r.gc[lanes].reshape(1, 256)
        b = r.bc[lanes].reshape(1, 256)
        for k in range(live):
            def step(y, carry):
                a0, a1, a2 = carry
                at = block(k, y)
                hat = (pre_c[pl.ds(at, SIDE), lanes] - centre) * inverse
                u = hat * g + b + fp[pl.ds(at, SIDE), lanes].astype(F32)
                s = 0.5 * jnp.tanh(0.5 * u) + 0.5
                h = u * s
                slope = s + (h - h * s)
                slope_c[pl.ds(at, SIDE), lanes] = slope
                return a0 + h, a1 + slope, a2 + slope * hat

            zero = jnp.zeros((SIDE, 256), F32)
            a0, a1, a2 = lax.fori_loop(0, height, step, (zero, zero, zero), unroll=height)
            p_row = (t.fold(a0) * (1.0 / area)).astype(BF16).astype(F32)
            to_dense(pool, 0, p_row, 8 * k + 2 * c)
            to_dense(slope_sum, k, t.fold(a1), 2 * c)
            to_dense(slope_hat, k, t.fold(a2), 2 * c)
    for k in range(live):
        pool[0, 24 + k : 25 + k, :] = jnp.full((1, 128), key[k], F32)
        pool[0, 28 + k : 29 + k, :] = jnp.full((1, 128), weight[k], F32)
    for q, device in enumerate(t.clip_peers):
        t.send(pool.at[0], pool.at[q + 1], r.pool_s.at[0], r.pool_r.at[0], device)
    turn(2)
    wait_bytes(pool.at[pl.ds(1, len(t.clip_peers))], r.pool_r.at[0])

    lw = dense_of(r.loss, r.dense)
    grads = []
    for k in range(live):
        my_key = jnp.full((1, 128), key[k], F32)
        my_weight = jnp.full((1, 128), weight[k], F32)
        mean = jnp.zeros((8, 128), F32)
        den = jnp.zeros((1, 128), F32)
        for q in range(len(t.clip_peers) + 1):
            for m in range(live):
                match = jnp.where(pool[q, 24 + m : 25 + m, :] == my_key, pool[q, 28 + m : 29 + m, :], 0.0)
                den = den + match
                mean = mean + match * pool[q, 8 * m : 8 * m + 8, :]
        den = jnp.where(den == 0.0, 1.0, den)
        mean = mean / den
        power = jnp.sum(jnp.sum(mean * mean, axis=0, keepdims=True), axis=1, keepdims=True)
        along = jnp.sum(jnp.sum(mean * lw, axis=0, keepdims=True), axis=1, keepdims=True)
        scale = lax.rsqrt(power * (1.0 / feat) + EPS)
        mean_grad = scale * (lw - (mean * scale) * (scale * along * (1.0 / feat)))
        grads.append((my_weight / den) * mean_grad * (1.0 / area))

    inv_c = r.inv_c[...]
    near3 = r.near[3]
    shift = jnp.zeros((8, 128), F32)
    gain = jnp.zeros((8, 128), F32)
    for k in range(live):
        shift = shift + grads[k] * slope_sum[k]
        gain = gain + grads[k] * slope_hat[k]
    near3[t.near_at(3), 0:8, :] = shift
    near3[t.near_at(3), 8:16, :] = gain
    t.near_send(3)
    coef, dense = r.coef, r.dense
    scale_c = dense_of(r.gc, dense) * inv_c
    for k in range(live):
        dense[...] = grads[k]
        row_form(coef, k, dense, 0, feat // 128)
        dense[...] = grads[k] * scale_c
        row_form(coef, 3 + k, dense, 0, feat // 128)
    t.sums_near(3)
    turn(3)
    both = t.sums_wide(3)
    r.vectors_c[...] = both
    dense[...] = both[0:8] * scale_c / n_all
    row_form(coef, 6, dense, 0, feat // 128)
    dense[...] = both[8:16] * scale_c * inv_c / n_all
    row_form(coef, 7, dense, 0, feat // 128)
    return n_all, inv_a, inv_b


def backward(t, n_all, inv_a, inv_b):
    r, live, mid, feat, rows, height = t.r, t.live, t.mid, t.feat, t.rows, t.height
    slots, width, quad, far, v, wc = t.slots, t.width, t.quad, t.far, t.v, r.wc
    coef, pre_c, slope_c, out = r.coef, r.pre_c, r.slope_c, r.vectors
    me, send = t.me, t.send
    gpc = r.gpc
    for k in range(live):
        for c in range(feat // 256):
            lanes = slice(c * 256, (c + 1) * 256)
            centre = r.table_c[0:1, lanes]
            c0 = coef[3 + k : 4 + k, lanes]
            c1 = coef[6:7, lanes] * v[k]
            c2 = coef[7:8, lanes] * v[k]

            def step(y, carry):
                at = block(k, y)
                grad = slope_c[pl.ds(at, SIDE), lanes] * c0 - (c1 + (pre_c[pl.ds(at, SIDE), lanes] - centre) * c2)
                gpc[pl.ds(at, SIDE), lanes] = grad.astype(BF16)
                return carry

            lax.fori_loop(0, height, step, 0, unroll=height)

    def back_sums(at, table, inv, grad_ref, slope_ref, pre_ref):
        zero = jnp.zeros((SIDE, mid), F32)
        carry = (zero, zero)
        centre = table[0:1, :]
        for k in range(live):
            def step(y, c):
                here = pl.ds(block(k, y), SIDE)
                grad = grad_ref[here, :] * slope_ref[here, :]
                grad_ref[here, :] = grad
                return c[0] + grad, c[1] + grad * (pre_ref[here, :] - centre)

            carry = lax.fori_loop(0, height, step, carry, unroll=height)
        buf = r.near[at]
        to_dense(buf, t.near_at(at), jnp.sum(carry[0], axis=0, keepdims=True), 0)
        to_dense(buf, t.near_at(at), jnp.sum(carry[1], axis=0, keepdims=True) * table[1:2, :], 2)

    def back_apply(at, table, gain_ref, inv, grad_ref, pre_ref, write):
        both = t.sums_wide(at)
        out[8 * at - 32 : 8 * at - 28, :] = both[0:4]
        dense = r.dense
        scale = dense_of(gain_ref, dense) * inv
        dense[0:2, :] = scale
        dense[2:4, :] = both[0:2] * scale / n_all
        dense[4:6, :] = both[2:4] * scale * inv / n_all
        for q in range(3):
            row_form(table, 2 + q, dense, 2 * q, 2)
        centre = table[0:1, :]
        for k in range(live):
            c0, c1, c2 = table[2:3, :], table[3:4, :] * v[k], table[4:5, :] * v[k]

            def step(y, carry):
                at_row = block(k, y)
                here = pl.ds(at_row, SIDE)
                write(at_row, grad_ref[here, :] * c0 - (c1 + (pre_ref[here, :] - centre) * c2))
                return carry

            lax.fori_loop(0, height, step, 0, unroll=height)

    core, bit_x, bit_y, at_z = me % 2, (me // 2) % 2, (me // 4) % 2, (me // 8) % quad
    at_far = me // (8 * quad)
    bit1 = bit_x + core * (bit_y - bit_x)
    bit2 = bit_y + core * (bit_x - bit_y)
    sibling = me + 1 - 2 * core
    peer1 = me + (1 - 2 * bit1) * (2 + 2 * core)
    peer2 = me + (1 - 2 * bit2) * (4 - 2 * core)
    z_at = flips(at_z, quad)
    z_peer = [me + 8 * (q - at_z) for q in z_at]
    far_peer = [me + 8 * quad * ((at_far + o) % far - at_far) for o in range(1, far)]
    chunk_s, chunk_r = r.chunk_s, r.chunk_r
    blocks = iter(ORDER)
    plan = [(0, q, 2) for q in range(2)] + [(1 + q, 0, 1) for q in range(3)] + [(4, q, 4) for q in range(4)]

    def chunk(q):
        name, at, count = plan[q]
        size = r.part[name].shape[0] // count
        part = r.part[name].at[pl.ds(at * size, size)]
        whole = (r.e, r.s0, r.s1, r.s2, r.r)[name].at[pl.ds(at * size, size)]
        half, quarter, eighth, piece = size // 2, size // 4, size // 8, size // (8 * quad)
        m8 = lambda value: pl.multiple_of(value, 8)
        at_h = m8(core * half)
        at_q = m8(at_h + bit1 * quarter)
        at_e = m8(at_q + bit2 * eighth)
        at_p = m8(at_e + at_z * piece)

        def go(step, src, dst, device):
            send(src, dst, chunk_s.at[q, step // 4], chunk_r.at[q, step], device)

        def finish(step, ref):
            wait_bytes(ref, chunk_r.at[q, step])

        rb0, rb1, rb2, rb3 = r.rb0[q], r.rb1[q], r.rb2[q], r.rb3[q]
        go(0, part.at[pl.ds(m8((1 - core) * half), half)], rb0, sibling)
        yield
        finish(0, rb0)
        part[pl.ds(at_h, half), :] = part[pl.ds(at_h, half), :] + rb0[...]
        go(1, part.at[pl.ds(m8(at_h + (1 - bit1) * quarter), quarter)], rb1, peer1)
        yield
        finish(1, rb1)
        part[pl.ds(at_q, quarter), :] = part[pl.ds(at_q, quarter), :] + rb1[...]
        go(2, part.at[pl.ds(m8(at_q + (1 - bit2) * eighth), eighth)], rb2, peer2)
        yield
        finish(2, rb2)
        part[pl.ds(at_e, eighth), :] = part[pl.ds(at_e, eighth), :] + rb2[...]
        for o in range(quad - 1):
            go(3, part.at[pl.ds(m8(at_e + z_at[o] * piece), piece)], rb3.at[pl.ds(o * piece, piece)], z_peer[o])
        yield
        finish(3, rb3)
        own = part[pl.ds(at_p, piece), :]
        for o in range(quad - 1):
            own = own + rb3[o * piece : (o + 1) * piece, :]
        if far > 1:
            rb4 = r.rb4[q]
            rb4[at_far] = own
            for device in far_peer:
                go(8, rb4.at[at_far], rb4.at[at_far], device)
            yield
            finish(8, rb4.at[pl.ds(0, far - 1)])
            own = rb4[0]
            for o in range(1, far):
                own = own + rb4[o]
        whole[pl.ds(at_p, piece), :] = own
        for o in range(quad - 1):
            go(4, whole.at[pl.ds(at_p, piece)], whole.at[pl.ds(at_p, piece)], z_peer[o])
        yield
        finish(4, whole.at[pl.ds(0, (quad - 1) * piece)])
        go(5, whole.at[pl.ds(at_e, eighth)], whole.at[pl.ds(at_e, eighth)], peer2)
        yield
        finish(5, whole.at[pl.ds(0, eighth)])
        go(6, whole.at[pl.ds(at_q, quarter)], whole.at[pl.ds(at_q, quarter)], peer1)
        yield
        finish(6, whole.at[pl.ds(0, quarter)])
        go(7, whole.at[pl.ds(at_h, half)], whole.at[pl.ds(at_h, half)], sibling)
        yield
        finish(7, whole.at[pl.ds(0, half)])
        yield

    chunks = [chunk(q) for q in range(len(plan))]

    def go_on(*which):
        for q in which:
            next(chunks[q])

    def go_on_all():
        go_on(*next(blocks))

    pre_a, slope_a, pre_b, slope_b, hbt, xt = r.pre_a, r.slope_a, r.pre_b, r.slope_b, r.hbt, r.xt
    we, wr, back = r.we, r.wr, r.back
    tiles = feat // 128
    group = SIDE // slots
    keep, moved, mask = t.keep, t.moved, t.mask
    grad_b, grad_a = r.grad_b, r.grad_a
    wait_bytes(wc, r.load_sem.at[15])
    g3 = r.g3

    def write_gb(at, grad):
        grad = jnp.where(mask, grad, 0.0)
        three(g3, at, pltpu.roll(grad, SIDE - 1, 0), grad, pltpu.roll(grad, 1, 0))

    def spatial_part(i):
        go_on_all()
        value = dot(xt[...], g3[(2 - i) * SIDE : (2 - i) * SIDE + rows, :])
        for j in range(3):
            r.part[1 + i][j * mid : (j + 1) * mid, :] = value[:, j * mid : (j + 1) * mid]
        go_on(2 + i)

    go_on_all()
    go_on_all()
    by_rows(grad_b, lambda here: dot(gpc[here, :], we[...], NT))
    back_sums(4, r.table_b, inv_b, grad_b, slope_b, pre_b)
    t.near_send(4)
    for e in range(2):
        go_on_all()
        for q in range(2 * e, 2 * e + 2):
            lanes = slice(q * 256, (q + 1) * 256)
            r.part[0][e * mid : (e + 1) * mid, q % 2 * 256 : (q % 2 + 1) * 256] = dot(hbt[...], gpc[:, lanes])
        go_on(e)
    t.sums_near(4)
    go_on_all()
    back_apply(4, r.table_b, r.gb, inv_b, grad_b, pre_b, write_gb)
    spatial_part(0)
    go_on_all()
    by_rows(
        grad_a, lambda here: sum(dot(g3[moved_rows(here, (2 - i) * SIDE), :], wc[i], NT) for i in range(3))
    )
    back_sums(5, r.table_a, inv_a, grad_a, slope_a, pre_a)
    t.near_send(5)
    spatial_part(1)
    t.sums_near(5)
    spatial_part(2)
    go_on_all()
    gpa = r.gpa

    def write_ga(at, grad):
        gpa[pl.ds(at, SIDE), :] = grad.astype(BF16)

    back_apply(5, r.table_a, r.ga, inv_a, grad_a, pre_a, write_ga)
    for q in range(4):
        go_on_all()
        r.part[4][q * 256 : (q + 1) * 256, :] = dot(r.ft[q * 256 : (q + 1) * 256, :], gpa[...])
        go_on(5 + q)

    go_on_all()
    by_rows(back, lambda here: dot(gpa[here, :], wr[...], NT))
    gf = r.gf

    def blend(y, carry):
        for p in range(tiles // group):
            values = []
            for q in range(group):
                lanes = slice((p * group + q) * 128, (p * group + q + 1) * 128)
                terms = [
                    slope_c[pl.ds(block(k, y), SIDE), lanes] * coef[k : k + 1, lanes]
                    + back[pl.ds(block(k, y), SIDE), lanes]
                    for k in range(live)
                ]
                values.append(terms[0] * keep[0])
                for m in range(1, live):
                    values.append(terms[m] * keep[m] + terms[m - 1] * moved[m - 1])
                values.append(terms[live - 1] * moved[live - 1])
            value = jnp.swapaxes(jnp.stack(values), 0, 1)
            gf[pl.ds(y * width, width), p * SIDE : (p + 1) * SIDE, :] = value[0:width].astype(BF16)
        return carry

    for q in range(height // 2):
        go_on_all()
        for y in range(2):
            blend(2 * q + y, 0)
    go_on_all()
    for each in chunks:
        for _ in each:
            pass

    t.all_sent(*range(7))
    wait_bytes(r.pool.at[pl.ds(1, len(t.clip_peers))], r.pool_s.at[0])
    for q, (name, _, count) in enumerate(plan):
        part = r.part[name]
        piece = part.shape[0] // count // (8 * quad)
        for m, pieces in enumerate((8 * quad - 1, 8 * quad - 1, far - 1)):
            if pieces:
                wait_bytes(part.at[pl.ds(0, pieces * piece)], chunk_s.at[q, m])


def store(gf, vectors_c, vectors, expand, s0, s1, s2, reduce, frames_out, reduce_out, spatial_out, expand_out, *rest):
    ga, ba, gb, bb, gc, bc, *scratch, sem = rest
    vectors_of = (
        (bc, vectors_c, 0), (gc, vectors_c, 8), (bb, vectors, 0), (gb, vectors, 2), (ba, vectors, 8), (ga, vectors, 10)
    )
    pltpu.make_async_copy(gf, frames_out, sem.at[0]).start()
    pltpu.make_async_copy(reduce, reduce_out, sem.at[1]).start()
    depth, width = expand_out.shape
    for q in range(2):
        pltpu.make_async_copy(
            expand.at[pl.ds(q * depth, depth)], expand_out.at[:, pl.ds(q * width // 2, width // 2)], sem.at[2]
        ).start()
    for i, part in enumerate((s0, s1, s2)):
        for j in range(3):
            pltpu.make_async_copy(part.at[pl.ds(j * depth, depth)], spatial_out.at[i, j], sem.at[3 + i]).start()
    for number, (ref, source, first) in enumerate(vectors_of):
        for q in range(ref.shape[0] // 128):
            scratch[number][q * 128 : (q + 1) * 128] = source[first + q : first + q + 1, :].reshape(128)
        pltpu.make_async_copy(scratch[number], ref, sem.at[6 + number]).start()
    wait_bytes(gf, sem.at[0])
    wait_bytes(reduce, sem.at[1])
    wait_bytes(expand, sem.at[2])
    for i, part in enumerate((s0, s1, s2)):
        wait_bytes(part, sem.at[3 + i])
    for number in range(6):
        wait_bytes(scratch[number], sem.at[6 + number])


def solution(mesh):
    n = mesh.shape["clip"]

    def shards(*args):
        slots, height, width, feat = args[0].shape
        mid = args[1].shape[1]
        rows = (slots - 1) * ROWS
        outer = n // 8
        quad = min(4, outer)
        far = outer // quad
        cfg = (n, slots, height, width, feat, mid)
        flat_shape = (height * width, slots * feat // 128, 128)
        hbm = pl.BlockSpec(memory_space=pltpu.HBM)
        vmem = pl.BlockSpec(memory_space=pltpu.VMEM)
        dma = pltpu.SemaphoreType.DMA
        depths = list(enumerate((5, 4, 8, 16, 4, 4, 8)))
        sizes = [(2 * mid, feat // 2)] + [(3 * mid, mid)] * 3 + [(feat, mid)]

        tiled = args[0].transpose(1, 2, 0, 3).reshape(height, width, slots, feat // 128, 128)
        tiled = tiled.transpose(0, 1, 3, 2, 4).reshape(flat_shape)
        given = [pltpu.with_memory_space_constraint(part, pltpu.HBM) for part in (tiled, *args[1:])]

        vm = pltpu.VMEM
        narrow, broad, square = vm((mid,), F32), vm((feat,), F32), vm((rows, mid), F32)
        ints = pltpu.SMEM((slots,), jnp.int32)
        plan = [(mid, feat // 2)] * 2 + [(3 * mid, mid)] * 3 + [(feat // 4, mid)] * 4
        outs = dict(
            gf=vm(flat_shape, BF16), vectors_c=vm((16, 128), F32), vectors=vm((16, 128), F32),
            **{name: vm(size, F32) for name, size in zip(dict(e=0, s0=0, s1=0, s2=0, r=0), sizes)},
        )
        scratch = dict(
            f4=vm((flat_shape[0] + SIDE - width, *flat_shape[1:]), BF16),
            fp=vm((rows, feat), BF16), ft=vm((feat, rows), BF16),
            wr=vm((feat, mid), BF16), ws=vm((3, 3, mid, mid), BF16), wc=vm((3, mid, 3 * mid), BF16), we=vm((mid, feat), BF16),
            valid=ints, clip=ints, segment=ints, share=pltpu.SMEM(args[13].shape, F32),
            ga=narrow, ba=narrow, gb=narrow, bb=narrow, gc=broad, bc=broad, loss=broad,
            xp=vm((rows + 2 * SIDE, 3 * mid), BF16), xt=vm((mid, rows), BF16),
            hb=vm((rows, mid), BF16), hbt=vm((mid, rows), BF16),
            pre_a=square, slope_a=square, pre_b=square, slope_b=square, grad_a=square, grad_b=square,
            pre_c=vm((rows, feat), F32), slope_c=vm((rows, feat), F32), back=vm((rows, feat), F32),
            gpc=vm((rows, feat), BF16), g3=vm((rows + 2 * SIDE, 3 * mid), BF16), gpa=vm((rows, mid), BF16),
            table_a=vm((8, mid), F32), table_b=vm((8, mid), F32),
            table_c=vm((8, feat), F32), coef=vm((8, feat), F32), dense=vm((8, 128), F32), inv_c=vm((8, 128), F32),
            pool=vm((6, 32, 128), F32), slope_sum=vm((3, 8, 128), F32), slope_hat=vm((3, 8, 128), F32),
            near=[vm((n if n <= 32 and at not in (2, 3, 6) else 8, deep, 128), F32) for at, deep in depths],
            wide=[vm((outer, deep, 128), F32) for at, deep in depths],
            plane=vm((outer, 8, 128), F32),
            part=[vm(size, F32) for size in sizes],
            rb0=[vm((size // 2, lanes), F32) for size, lanes in plan],
            rb1=[vm((size // 4, lanes), F32) for size, lanes in plan],
            rb2=[vm((size // 8, lanes), F32) for size, lanes in plan],
            rb3=[vm(((quad - 1) * size // (8 * quad), lanes), F32) for size, lanes in plan],
            rb4=[vm((far, size // (8 * quad), lanes), F32) for size, lanes in plan if far > 1],
            load_sem=dma((16,)), near_s=dma((7,)), near_r=dma((7,)), wide_s=dma((7,)), wide_r=dma((7,)),
            pool_s=dma((1,)), pool_r=dma((1,)), chunk_s=dma((9, 3)), chunk_r=dma((9, 9)),
        )
        names = (*arg_names(), *outs, *scratch)

        def kernel(*refs):
            t = Step(cfg, SimpleNamespace(**dict(zip(names, refs, strict=True))))
            prologue(t)
            backward(t, *forward(t))

        results = pl.pallas_call(
            kernel,
            out_shape=list(outs.values()),
            in_specs=[hbm] * len(given),
            out_specs=[vmem] * len(outs),
            scratch_shapes=list(scratch.values()),
            compiler_params=pltpu.CompilerParams(
                collective_id=0, has_side_effects=True, vmem_limit_bytes=50 * 1024 * 1024
            ),
        )(*given)
        vector = jax.ShapeDtypeStruct((mid,), F32)
        wide_vector = jax.ShapeDtypeStruct((feat,), F32)
        flat_grad, *rest = pl.pallas_call(
            store,
            out_shape=[
                jax.ShapeDtypeStruct(flat_shape, BF16),
                jax.ShapeDtypeStruct((feat, mid), F32),
                jax.ShapeDtypeStruct((3, 3, mid, mid), F32),
                jax.ShapeDtypeStruct((mid, feat), F32),
                vector, vector, vector, vector, wide_vector, wide_vector,
            ],
            in_specs=[vmem] * 8,
            out_specs=[hbm] * 10,
            scratch_shapes=[*(vm((c,), F32) for c in (feat, feat, mid, mid, mid, mid)), dma((12,))],
            compiler_params=pltpu.CompilerParams(vmem_limit_bytes=8 * 1024 * 1024),
        )(*(pltpu.with_memory_space_constraint(part, pltpu.VMEM) for part in results))
        grad_frames = flat_grad.reshape(height, width, feat // 128, slots, 128).transpose(0, 1, 3, 2, 4)
        return grad_frames.reshape(height, width, slots, feat).transpose(2, 0, 1, 3), *rest

    split = P("clip")
    in_specs = (split,) + (P(),) * 9 + (split,) * 3 + (P(), P())
    out_specs = (split,) + (P(),) * 9
    return jax.shard_map(shards, mesh=mesh, in_specs=in_specs, out_specs=out_specs, check_vma=False)


def arg_names():
    return dict(
        frames=0, w_reduce=0, w_spatial=0, w_expand=0, gain_a=0, bias_a=0, gain_b=0, bias_b=0, gain_c=0, bias_c=0,
        clip_ids=0, segment_ids=0, slot_valid=0, segment_weight=0, loss_weight=0,
    )
```

profile of v0, /device:TPU:0, one launch (start us, length us, event | category | flops | bytes accessed | tf_op | source)
XLA Modules:
  0.0 98.3 jit_solution(9939556810278109047)
XLA Ops:
  0.6 95.0 %shard_map.222 = (bf16[196,32,128]{2,1,0:T(8,128)(2,1)S(1)}, f32[16,128]{1,0:T(8,128)S(1)}, f32[16,128]{1,0:T(8,128)S(1)}, f32[512,512]{1,0:T(8,128)S(1)}, f32[7...) custom-call(bf16[196,32,128]{2,1,0:T(8,128)(2,1)} %bitcast.14, ...), custom_call_target="tpu_custom_call" | custom-call | tf_op jit(solution)/shard_map/pallas_call | solution.py:833
  95.6 2.7 %shard_map.223 = (bf16[196,32,128]{2,1,0:T(8,128)(2,1)}, f32[1024,256]{1,0:T(8,128)}, f32[3,3,256,256]{3,2,1,0:T(8,128)}, f32[256,1024]{1,0:T(8,128)}, f32[256]{...) custom-call(bf16[196,32,128]{2,1,0:T(8,128)(2,1)S(1)} %get-tuple-element.28.gf, ...), custom_call_target="tpu_custom_call" | custom-call | tf_op jit(solution)/shard_map/pallas_call | solution.py:845
where the time goes:
time: 98.5 us; the launch traced here: 98.3 us
  Pallas kernels  97.6 us (99%)
    pallas_call x1, Pallas kernels, shards(): pl.pallas_call(kernel, out_shape=list(outs.values()), in_specs=[hbm] * le...  95 us
    pallas_call x1, Pallas kernels, shards(): pl.pallas_call(store, out_shape=[jax.ShapeDtypeStruct(flat_shape, BF16),...  2.69 us

commit v1 on v0

--- a/solution.py
+++ b/solution.py
@@ -23,24 +23,24 @@
     (),
     (),
     (),
+    (0, 1,),
     (),
-    (0, 1,),
-    (2, 0,),
     (1,),
-    (2, 0, 1, 3,),
-    (2, 4,),
+    (0,),
+    (2, 1,),
+    (3, 0,),
     (),
-    (),
-    (0,),
-    (1, 3, 5, 2, 4,),
-    (6, 3, 8,),
-    (1, 0, 5, 7, 4, 8, 1, 3, 6, 7, 8, 2, 0,),
-    (4, 7, 3,),
-    (6, 2, 8, 1, 5, 0, 4, 7, 3, 6, 8, 5, 7, 1, 6, 4,),
-    (5, 6, 0, 3,),
-    (7,),
-    (8, 2, 4, 5, 7, 8, 6, 3, 5,),
-    (7, 8, 6, 5, 4, 2,),
+    (1, 2, 6, 0, 3, 5,),
+    (2, 1, 6, 4,),
+    (3, 0,),
+    (6, 5, 2, 7, 4, 3, 8, 0, 5, 7,),
+    (2, 4, 8, 1, 7, 3, 5, 6, 2, 8, 4, 5, 3, 8, 7, 6, 2, 5, 4, 7, 8, 6, 4, 3,),
+    (7, 0,),
+    (5, 1, 8,),
+    (6, 4, 7, 0, 3,),
+    (8, 5,),
+    (7, 2, 4,),
+    (8, 6, 1,),
 )
 
 
@@ -436,31 +436,34 @@
             zero = jnp.zeros((SIDE, 256), F32)
             a0, a1, a2 = lax.fori_loop(0, height, step, (zero, zero, zero), unroll=height)
             p_row = (t.fold(a0) * (1.0 / area)).astype(BF16).astype(F32)
-            to_dense(pool, 0, p_row, 8 * k + 2 * c)
+            to_dense(pool[h], 0, p_row, 4 * k + 2 * (c - 2 * h))
             to_dense(slope_sum, k, t.fold(a1), 2 * c)
             to_dense(slope_hat, k, t.fold(a2), 2 * c)
-    for k in range(live):
-        pool[0, 24 + k : 25 + k, :] = jnp.full((1, 128), key[k], F32)
-        pool[0, 28 + k : 29 + k, :] = jnp.full((1, 128), weight[k], F32)
-    for q, device in enumerate(t.clip_peers):
-        t.send(pool.at[0], pool.at[q + 1], r.pool_s.at[0], r.pool_r.at[0], device)
+        if (c + 1) * 256 % half == 0:
+            for k in range(live):
+                pool[h][0, 12 + k : 13 + k, :] = jnp.full((1, 128), (key, weight)[h][k], F32)
+            for q, device in enumerate(t.clip_peers):
+                t.send(pool[h].at[0], pool[h].at[q + 1], r.pool_s.at[h], r.pool_r.at[h], device)
     turn(2)
-    wait_bytes(pool.at[pl.ds(1, len(t.clip_peers))], r.pool_r.at[0])
+    for h in range(2):
+        wait_bytes(pool[h].at[pl.ds(1, len(t.clip_peers))], r.pool_r.at[h])
 
     lw = dense_of(r.loss, r.dense)
     grads = []
     for k in range(live):
         my_key = jnp.full((1, 128), key[k], F32)
         my_weight = jnp.full((1, 128), weight[k], F32)
-        mean = jnp.zeros((8, 128), F32)
+        parts = [jnp.zeros((4, 128), F32)] * 2
         den = jnp.zeros((1, 128), F32)
         for q in range(len(t.clip_peers) + 1):
             for m in range(live):
-                match = jnp.where(pool[q, 24 + m : 25 + m, :] == my_key, pool[q, 28 + m : 29 + m, :], 0.0)
+                match = jnp.where(pool[0][q, 12 + m : 13 + m, :] == my_key, pool[1][q, 12 + m : 13 + m, :], 0.0)
                 den = den + match
-                mean = mean + match * pool[q, 8 * m : 8 * m + 8, :]
+                parts = [parts[h] + match * pool[h][q, 4 * m : 4 * m + 4, :] for h in range(2)]
         den = jnp.where(den == 0.0, 1.0, den)
-        mean = mean / den
+        for h in range(2):
+            r.clip_mean[k, 4 * h : 4 * h + 4, :] = parts[h] / den
+        mean = r.clip_mean[k]
         power = jnp.sum(jnp.sum(mean * mean, axis=0, keepdims=True), axis=1, keepdims=True)
         along = jnp.sum(jnp.sum(mean * lw, axis=0, keepdims=True), axis=1, keepdims=True)
         scale = lax.rsqrt(power * (1.0 / feat) + EPS)
@@ -676,13 +679,13 @@
     t.sums_near(4)
     go_on_all()
     back_apply(4, r.table_b, r.gb, inv_b, grad_b, pre_b, write_gb)
-    spatial_part(0)
     go_on_all()
     by_rows(
         grad_a, lambda here: sum(dot(g3[moved_rows(here, (2 - i) * SIDE), :], wc[i], NT) for i in range(3))
     )
     back_sums(5, r.table_a, inv_a, grad_a, slope_a, pre_a)
     t.near_send(5)
+    spatial_part(0)
     spatial_part(1)
     t.sums_near(5)
     spatial_part(2)
@@ -730,7 +733,8 @@
             pass
 
     t.all_sent(*range(7))
-    wait_bytes(r.pool.at[pl.ds(1, len(t.clip_peers))], r.pool_s.at[0])
+    for h in range(2):
+        wait_bytes(r.pool[h].at[pl.ds(1, len(t.clip_peers))], r.pool_s.at[h])
     for q, (name, _, count) in enumerate(plan):
         part = r.part[name]
         piece = part.shape[0] // count // (8 * quad)
@@ -810,7 +814,7 @@
             gpc=vm((rows, feat), BF16), g3=vm((rows + 2 * SIDE, 3 * mid), BF16), gpa=vm((rows, mid), BF16),
             table_a=vm((8, mid), F32), table_b=vm((8, mid), F32),
             table_c=vm((8, feat), F32), coef=vm((8, feat), F32), dense=vm((8, 128), F32), inv_c=vm((8, 128), F32),
-            pool=vm((6, 32, 128), F32), slope_sum=vm((3, 8, 128), F32), slope_hat=vm((3, 8, 128), F32),
+            pool=[vm((6, 16, 128), F32)] * 2, clip_mean=vm((3, 8, 128), F32), slope_sum=vm((3, 8, 128), F32), slope_hat=vm((3, 8, 128), F32),
             near=[vm((n if n <= 32 and at not in (2, 3, 6) else 8, deep, 128), F32) for at, deep in depths],
             wide=[vm((outer, deep, 128), F32) for at, deep in depths],
             plane=vm((outer, 8, 128), F32),
@@ -821,7 +825,7 @@
             rb3=[vm(((quad - 1) * size // (8 * quad), lanes), F32) for size, lanes in plan],
             rb4=[vm((far, size // (8 * quad), lanes), F32) for size, lanes in plan if far > 1],
             load_sem=dma((16,)), near_s=dma((7,)), near_r=dma((7,)), wide_s=dma((7,)), wide_r=dma((7,)),
-            pool_s=dma((1,)), pool_r=dma((1,)), chunk_s=dma((9, 3)), chunk_r=dma((9, 9)),
+            pool_s=dma((2,)), pool_r=dma((2,)), chunk_s=dma((9, 3)), chunk_r=dma((9, 9)),
         )
         names = (*arg_names(), *outs, *scratch)
 

time: 98.5 us -> 99.6 us (1.011)
  Pallas kernels: 97.6 us -> 98.8 us
    pallas_call x1, Pallas kernels: 95 us -> 96.1 us  [shards(): pl.pallas_call(kernel, out_shape=list(outs.values()), in_specs=[hbm] * le...]
where the time goes in v1:
time: 99.6 us; the launch traced here: 99.4 us
  Pallas kernels  98.8 us (99%)
    pallas_call x1, Pallas kernels, shards(): pl.pallas_call(kernel, out_shape=list(outs.values()), in_specs=[hbm] * le...  96.1 us
    pallas_call x1, Pallas kernels, shards(): pl.pallas_call(store, out_shape=[jax.ShapeDtypeStruct(flat_shape, BF16),...  2.69 us

profile of v1, /device:TPU:0, one launch (start us, length us, event | category | flops | bytes accessed | tf_op | source)
XLA Modules:
  0.0 99.4 jit_solution(240128766388631119)
XLA Ops:
  0.6 96.1 %shard_map.222 = (bf16[196,32,128]{2,1,0:T(8,128)(2,1)S(1)}, f32[16,128]{1,0:T(8,128)S(1)}, f32[16,128]{1,0:T(8,128)S(1)}, f32[512,512]{1,0:T(8,128)S(1)}, f32[7...) custom-call(bf16[196,32,128]{2,1,0:T(8,128)(2,1)} %bitcast.14, ...), custom_call_target="tpu_custom_call" | custom-call | tf_op jit(solution)/shard_map/pallas_call | solution.py:837
  96.7 2.7 %shard_map.223 = (bf16[196,32,128]{2,1,0:T(8,128)(2,1)}, f32[1024,256]{1,0:T(8,128)}, f32[3,3,256,256]{3,2,1,0:T(8,128)}, f32[256,1024]{1,0:T(8,128)}, f32[256]{...) custom-call(bf16[196,32,128]{2,1,0:T(8,128)(2,1)S(1)} %get-tuple-element.28.gf, ...), custom_call_target="tpu_custom_call" | custom-call | tf_op jit(solution)/shard_map/pallas_call | solution.py:849

commit v2 on v0

--- a/solution.py
+++ b/solution.py
@@ -307,27 +307,16 @@
 
 def prologue(t):
     r, slots, live, width, feat = t.r, t.slots, t.live, t.width, t.feat
-    t.places()
-    t.greet()
     t.load(
         frames=(r.frames, r.f4.at[pl.ds(0, t.area)]), valid=(r.slot_valid, r.valid), reduce=(r.w_reduce, r.wr)
     )
+    t.places()
+    t.greet()
     r.f4[t.area :] = jnp.zeros((r.f4.shape[0] - t.area, *r.f4.shape[1:]), BF16)
     clear(r.fp)
     t.loaded(valid=0)
     t.slot_facts()
     t.loaded(frames=0)
-    t.load(
-        clip=(r.clip_ids, r.clip), segment=(r.segment_ids, r.segment),
-        share=(r.segment_weight, r.share), spatial=(r.w_spatial, r.ws), expand=(r.w_expand, r.we),
-        ga=(r.gain_a, r.ga), ba=(r.bias_a, r.ba), gb=(r.gain_b, r.gb), bb=(r.bias_b, r.bb),
-        gc=(r.gain_c, r.gc), bc=(r.bias_c, r.bc), loss=(r.loss_weight, r.loss),
-    )
-    for i in range(3):
-        for j in range(3):
-            pltpu.make_async_copy(
-                r.w_spatial.at[i, j], r.wc.at[i, :, pl.ds(j * t.mid, t.mid)], r.load_sem.at[15]
-            ).start()
     fp, f4 = r.fp, r.f4
     tiles = feat // 128
     group = SIDE // slots
@@ -360,6 +349,17 @@
 
     t.all_here()
     t.near_send(0)
+    t.load(
+        clip=(r.clip_ids, r.clip), segment=(r.segment_ids, r.segment),
+        share=(r.segment_weight, r.share), spatial=(r.w_spatial, r.ws), expand=(r.w_expand, r.we),
+        ga=(r.gain_a, r.ga), ba=(r.bias_a, r.ba), gb=(r.gain_b, r.gb), bb=(r.bias_b, r.bb),
+        gc=(r.gain_c, r.gc), bc=(r.bias_c, r.bc), loss=(r.loss_weight, r.loss),
+    )
+    for i in range(3):
+        for j in range(3):
+            pltpu.make_async_copy(
+                r.w_spatial.at[i, j], r.wc.at[i, :, pl.ds(j * mid, mid)], r.load_sem.at[15]
+            ).start()
     turn(0)
     t.stats_near(0, mid // 128)
     clear(r.xp, r.hb, r.g3, r.gpc, r.gpa)
@@ -724,13 +724,13 @@
         go_on_all()
         for y in range(2):
             blend(2 * q + y, 0)
+    t.all_sent(*range(7))
+    wait_bytes(r.pool.at[pl.ds(1, len(t.clip_peers))], r.pool_s.at[0])
     go_on_all()
     for each in chunks:
         for _ in each:
             pass
 
-    t.all_sent(*range(7))
-    wait_bytes(r.pool.at[pl.ds(1, len(t.clip_peers))], r.pool_s.at[0])
     for q, (name, _, count) in enumerate(plan):
         part = r.part[name]
         piece = part.shape[0] // count // (8 * quad)

time: 98.5 us -> 98.5 us (level)
  no operation moved by 1% of the time
where the time goes in v2:
time: 98.5 us; the launch traced here: 98.3 us
  Pallas kernels  97.7 us (99%)
    pallas_call x1, Pallas kernels, shards(): pl.pallas_call(kernel, out_shape=list(outs.values()), in_specs=[hbm] * le...  95 us
    pallas_call x1, Pallas kernels, shards(): pl.pallas_call(store, out_shape=[jax.ShapeDtypeStruct(flat_shape, BF16),...  2.69 us

profile of v2, /device:TPU:0, one launch (start us, length us, event | category | flops | bytes accessed | tf_op | source)
XLA Modules:
  0.0 98.3 jit_solution(2183617993411459131)
XLA Ops:
  0.6 95.0 %shard_map.222 = (bf16[196,32,128]{2,1,0:T(8,128)(2,1)S(1)}, f32[16,128]{1,0:T(8,128)S(1)}, f32[16,128]{1,0:T(8,128)S(1)}, f32[512,512]{1,0:T(8,128)S(1)}, f32[7...) custom-call(bf16[196,32,128]{2,1,0:T(8,128)(2,1)} %bitcast.14, ...), custom_call_target="tpu_custom_call" | custom-call | tf_op jit(solution)/shard_map/pallas_call | solution.py:833
  95.6 2.7 %shard_map.223 = (bf16[196,32,128]{2,1,0:T(8,128)(2,1)}, f32[1024,256]{1,0:T(8,128)}, f32[3,3,256,256]{3,2,1,0:T(8,128)}, f32[256,1024]{1,0:T(8,128)}, f32[256]{...) custom-call(bf16[196,32,128]{2,1,0:T(8,128)(2,1)S(1)} %get-tuple-element.28.gf, ...), custom_call_target="tpu_custom_call" | custom-call | tf_op jit(solution)/shard_map/pallas_call | solution.py:845

commit v3 on v2

--- a/solution.py
+++ b/solution.py
@@ -283,21 +283,23 @@
 def combine(buf, counts, group, count):
     n_part = [counts(q) for q in range(group)]
     s_part = [buf[q, 0:count, :] for q in range(group)]
-    n_all = sum(n_part[1:], n_part[0])
-    s_all = sum(s_part[1:], s_part[0])
+    n_all, s_all = tree(n_part), tree(s_part)
     mean = s_all / jnp.maximum(n_all, 1.0)
-    spread = jnp.zeros((count, 128), F32)
+    spread = []
     for q in range(group):
         gap = s_part[q] / jnp.maximum(n_part[q], 1.0) - mean
-        spread = spread + (buf[q, count : 2 * count, :] + n_part[q] * gap * gap)
-    return n_all, s_all, mean, spread
+        spread.append(buf[q, count : 2 * count, :] + n_part[q] * gap * gap)
+    return n_all, s_all, mean, tree(spread)
+
+
+def tree(values):
+    while len(values) > 1:
+        values = [sum(values[q + 1 : q + 2], values[q]) for q in range(0, len(values), 2)]
+    return values[0]
 
 
 def total(buf):
-    out = buf[0]
-    for q in range(1, buf.shape[0]):
-        out = out + buf[q]
-    return out
+    return tree([buf[q] for q in range(buf.shape[0])])
 
 
 def clear(*refs):
@@ -436,31 +438,34 @@
             zero = jnp.zeros((SIDE, 256), F32)
             a0, a1, a2 = lax.fori_loop(0, height, step, (zero, zero, zero), unroll=height)
             p_row = (t.fold(a0) * (1.0 / area)).astype(BF16).astype(F32)
-            to_dense(pool, 0, p_row, 8 * k + 2 * c)
+            to_dense(pool[h], 0, p_row, 4 * k + 2 * (c - 2 * h))
             to_dense(slope_sum, k, t.fold(a1), 2 * c)
             to_dense(slope_hat, k, t.fold(a2), 2 * c)
-    for k in range(live):
-        pool[0, 24 + k : 25 + k, :] = jnp.full((1, 128), key[k], F32)
-        pool[0, 28 + k : 29 + k, :] = jnp.full((1, 128), weight[k], F32)
-    for q, device in enumerate(t.clip_peers):
-        t.send(pool.at[0], pool.at[q + 1], r.pool_s.at[0], r.pool_r.at[0], device)
+        if (c + 1) * 256 % half == 0:
+            for k in range(live):
+                pool[h][0, 12 + k : 13 + k, :] = jnp.full((1, 128), (key, weight)[h][k], F32)
+            for q, device in enumerate(t.clip_peers):
+                t.send(pool[h].at[0], pool[h].at[q + 1], r.pool_s.at[h], r.pool_r.at[h], device)
     turn(2)
-    wait_bytes(pool.at[pl.ds(1, len(t.clip_peers))], r.pool_r.at[0])
+    for h in range(2):
+        wait_bytes(pool[h].at[pl.ds(1, len(t.clip_peers))], r.pool_r.at[h])
 
     lw = dense_of(r.loss, r.dense)
     grads = []
     for k in range(live):
         my_key = jnp.full((1, 128), key[k], F32)
         my_weight = jnp.full((1, 128), weight[k], F32)
-        mean = jnp.zeros((8, 128), F32)
+        parts = [jnp.zeros((4, 128), F32)] * 2
         den = jnp.zeros((1, 128), F32)
         for q in range(len(t.clip_peers) + 1):
             for m in range(live):
-                match = jnp.where(pool[q, 24 + m : 25 + m, :] == my_key, pool[q, 28 + m : 29 + m, :], 0.0)
+                match = jnp.where(pool[0][q, 12 + m : 13 + m, :] == my_key, pool[1][q, 12 + m : 13 + m, :], 0.0)
                 den = den + match
-                mean = mean + match * pool[q, 8 * m : 8 * m + 8, :]
+                parts = [parts[h] + match * pool[h][q, 4 * m : 4 * m + 4, :] for h in range(2)]
         den = jnp.where(den == 0.0, 1.0, den)
-        mean = mean / den
+        for h in range(2):
+            r.clip_mean[k, 4 * h : 4 * h + 4, :] = parts[h] / den
+        mean = r.clip_mean[k]
         power = jnp.sum(jnp.sum(mean * mean, axis=0, keepdims=True), axis=1, keepdims=True)
         along = jnp.sum(jnp.sum(mean * lw, axis=0, keepdims=True), axis=1, keepdims=True)
         scale = lax.rsqrt(power * (1.0 / feat) + EPS)
@@ -725,7 +730,8 @@
         for y in range(2):
             blend(2 * q + y, 0)
     t.all_sent(*range(7))
-    wait_bytes(r.pool.at[pl.ds(1, len(t.clip_peers))], r.pool_s.at[0])
+    for h in range(2):
+        wait_bytes(r.pool[h].at[pl.ds(1, len(t.clip_peers))], r.pool_s.at[h])
     go_on_all()
     for each in chunks:
         for _ in each:
@@ -810,7 +816,7 @@
             gpc=vm((rows, feat), BF16), g3=vm((rows + 2 * SIDE, 3 * mid), BF16), gpa=vm((rows, mid), BF16),
             table_a=vm((8, mid), F32), table_b=vm((8, mid), F32),
             table_c=vm((8, feat), F32), coef=vm((8, feat), F32), dense=vm((8, 128), F32), inv_c=vm((8, 128), F32),
-            pool=vm((6, 32, 128), F32), slope_sum=vm((3, 8, 128), F32), slope_hat=vm((3, 8, 128), F32),
+            pool=[vm((6, 16, 128), F32)] * 2, clip_mean=vm((3, 8, 128), F32), slope_sum=vm((3, 8, 128), F32), slope_hat=vm((3, 8, 128), F32),
             near=[vm((n if n <= 32 and at not in (2, 3, 6) else 8, deep, 128), F32) for at, deep in depths],
             wide=[vm((outer, deep, 128), F32) for at, deep in depths],
             plane=vm((outer, 8, 128), F32),
@@ -821,7 +827,7 @@
             rb3=[vm(((quad - 1) * size // (8 * quad), lanes), F32) for size, lanes in plan],
             rb4=[vm((far, size // (8 * quad), lanes), F32) for size, lanes in plan if far > 1],
             load_sem=dma((16,)), near_s=dma((7,)), near_r=dma((7,)), wide_s=dma((7,)), wide_r=dma((7,)),
-            pool_s=dma((1,)), pool_r=dma((1,)), chunk_s=dma((9, 3)), chunk_r=dma((9, 9)),
+            pool_s=dma((2,)), pool_r=dma((2,)), chunk_s=dma((9, 3)), chunk_r=dma((9, 9)),
         )
         names = (*arg_names(), *outs, *scratch)
 

time: 98.5 us -> 98.4 us (level)
  no operation moved by 1% of the time
where the time goes in v3:
time: 98.4 us; the launch traced here: 98.2 us
  Pallas kernels  97.6 us (99%)
    pallas_call x1, Pallas kernels, shards(): pl.pallas_call(kernel, out_shape=list(outs.values()), in_specs=[hbm] * le...  94.9 us
    pallas_call x1, Pallas kernels, shards(): pl.pallas_call(store, out_shape=[jax.ShapeDtypeStruct(flat_shape, BF16),...  2.69 us

profile of v3, /device:TPU:0, one launch (start us, length us, event | category | flops | bytes accessed | tf_op | source)
XLA Modules:
  0.0 98.2 jit_solution(3924642851602168342)
XLA Ops:
  0.6 94.9 %shard_map.222 = (bf16[196,32,128]{2,1,0:T(8,128)(2,1)S(1)}, f32[16,128]{1,0:T(8,128)S(1)}, f32[16,128]{1,0:T(8,128)S(1)}, f32[512,512]{1,0:T(8,128)S(1)}, f32[7...) custom-call(bf16[196,32,128]{2,1,0:T(8,128)(2,1)} %bitcast.14, ...), custom_call_target="tpu_custom_call" | custom-call | tf_op jit(solution)/shard_map/pallas_call | solution.py:839
  95.5 2.7 %shard_map.223 = (bf16[196,32,128]{2,1,0:T(8,128)(2,1)}, f32[1024,256]{1,0:T(8,128)}, f32[3,3,256,256]{3,2,1,0:T(8,128)}, f32[256,1024]{1,0:T(8,128)}, f32[256]{...) custom-call(bf16[196,32,128]{2,1,0:T(8,128)(2,1)S(1)} %get-tuple-element.28.gf, ...), custom_call_target="tpu_custom_call" | custom-call | tf_op jit(solution)/shard_map/pallas_call | solution.py:851

commit v4 on v0

--- a/solution.py
+++ b/solution.py
@@ -307,10 +307,12 @@
 
 def prologue(t):
     r, slots, live, width, feat = t.r, t.slots, t.live, t.width, t.feat
+    early = (t.height // 2 + 1) * t.width
     t.places()
     t.greet()
     t.load(
-        frames=(r.frames, r.f4.at[pl.ds(0, t.area)]), valid=(r.slot_valid, r.valid), reduce=(r.w_reduce, r.wr)
+        frames=(r.frames.at[pl.ds(0, early)], r.f4.at[pl.ds(0, early)]), valid=(r.slot_valid, r.valid), reduce=(r.w_reduce, r.wr),
+        rest=(r.frames.at[pl.ds(early, t.area - early)], r.f4.at[pl.ds(early, t.area - early)]),
     )
     r.f4[t.area :] = jnp.zeros((r.f4.shape[0] - t.area, *r.f4.shape[1:]), BF16)
     clear(r.fp)
@@ -326,7 +328,7 @@
     for i in range(3):
         for j in range(3):
             pltpu.make_async_copy(
-                r.w_spatial.at[i, j], r.wc.at[i, :, pl.ds(j * t.mid, t.mid)], r.load_sem.at[15]
+                r.w_spatial.at[i, j], r.wc.at[i, :, pl.ds(j * t.mid, t.mid)], r.load_sem.at[16]
             ).start()
     fp, f4 = r.fp, r.f4
     tiles = feat // 128
@@ -344,7 +346,9 @@
                     fp[pl.ds(block(k, y), SIDE), lanes] = jnp.where(short, row, 0.0).astype(BF16)
         return carry
 
-    lax.fori_loop(0, t.height, regroup, 0)
+    lax.fori_loop(0, t.height // 2, regroup, 0)
+    t.loaded(rest=0)
+    lax.fori_loop(t.height // 2, t.height, regroup, 0)
     t.loaded(reduce=0)
     by_rows(r.pre_a, lambda here: dot(fp[here, :], r.wr[...]))
     t.local_stats(r.near[0], t.near_at(0), r.pre_a)
@@ -648,7 +652,7 @@
     group = SIDE // slots
     keep, moved, mask = t.keep, t.moved, t.mask
     grad_b, grad_a = r.grad_b, r.grad_a
-    wait_bytes(wc, r.load_sem.at[15])
+    wait_bytes(wc, r.load_sem.at[16])
     g3 = r.g3
 
     def write_gb(at, grad):
@@ -820,7 +824,7 @@
             rb2=[vm((size // 8, lanes), F32) for size, lanes in plan],
             rb3=[vm(((quad - 1) * size // (8 * quad), lanes), F32) for size, lanes in plan],
             rb4=[vm((far, size // (8 * quad), lanes), F32) for size, lanes in plan if far > 1],
-            load_sem=dma((16,)), near_s=dma((7,)), near_r=dma((7,)), wide_s=dma((7,)), wide_r=dma((7,)),
+            load_sem=dma((17,)), near_s=dma((7,)), near_r=dma((7,)), wide_s=dma((7,)), wide_r=dma((7,)),
             pool_s=dma((1,)), pool_r=dma((1,)), chunk_s=dma((9, 3)), chunk_r=dma((9, 9)),
         )
         names = (*arg_names(), *outs, *scratch)

time: 98.5 us -> 98.5 us (level)
  no operation moved by 1% of the time
where the time goes in v4:
time: 98.5 us; the launch traced here: 98.3 us
  Pallas kernels  97.7 us (99%)
    pallas_call x1, Pallas kernels, shards(): pl.pallas_call(kernel, out_shape=list(outs.values()), in_specs=[hbm] * le...  95 us
    pallas_call x1, Pallas kernels, shards(): pl.pallas_call(store, out_shape=[jax.ShapeDtypeStruct(flat_shape, BF16),...  2.69 us

profile of v4, /device:TPU:0, one launch (start us, length us, event | category | flops | bytes accessed | tf_op | source)
XLA Modules:
  0.0 98.3 jit_solution(17916899959388177927)
XLA Ops:
  0.6 95.0 %shard_map.222 = (bf16[196,32,128]{2,1,0:T(8,128)(2,1)S(1)}, f32[16,128]{1,0:T(8,128)S(1)}, f32[16,128]{1,0:T(8,128)S(1)}, f32[512,512]{1,0:T(8,128)S(1)}, f32[7...) custom-call(bf16[196,32,128]{2,1,0:T(8,128)(2,1)} %bitcast.14, ...), custom_call_target="tpu_custom_call" | custom-call | tf_op jit(solution)/shard_map/pallas_call | solution.py:837
  95.6 2.7 %shard_map.223 = (bf16[196,32,128]{2,1,0:T(8,128)(2,1)}, f32[1024,256]{1,0:T(8,128)}, f32[3,3,256,256]{3,2,1,0:T(8,128)}, f32[256,1024]{1,0:T(8,128)}, f32[256]{...) custom-call(bf16[196,32,128]{2,1,0:T(8,128)(2,1)S(1)} %get-tuple-element.28.gf, ...), custom_call_target="tpu_custom_call" | custom-call | tf_op jit(solution)/shard_map/pallas_call | solution.py:849
